TPU v7x, 32 devices: a whole 2x2x4 slice. The times are simulated.
32 devices in a mesh: row: 8 (over z, y), col: 4 (over x, core).
Axes of the slice: x: 2, y: 2, z: 4, core: 2. Of those that a mesh axis runs over, the one named last changes fastest.
Arguments:
- markov: bfloat16 [128, 512, 64], P(('row', 'col')), may hold values from -14 to 14, as said below
- probes: bfloat16 [16, 1024], P(None, 'col'), may hold values from -0.1875 to 0.1875
Outputs:
- range_basis: bfloat16 [16, 65536], P(None, ('row', 'col'))
- projected: float32 [16, 1024], P(None, 'col')
Inputs may be any that keep to these rules, and one draw needn't show every extreme that they name: `markov`: markov blocks of a measured response.
All inputs are finite; a program needn't handle non-finite values.
Results may differ from a plain program's by a relative error of at most 0.0049.
Values may be sent and summed in bfloat16 or wider, within the bound.
A program may use at most 64 MiB of HBM per device.

v0:
```python
import math

import jax
import jax.numpy as jnp
from jax import lax
from jax.sharding import PartitionSpec as P


def passed_along(x, axis, by):
    peers = lax.axis_size(axis)
    pairs = [(i, i + by) for i in range(peers) if 0 <= i + by < peers]
    return lax.ppermute(x, axis, pairs)


def on_device(markov, probes):
    blocks_dev = markov.shape[0]
    sensors = markov.shape[1]
    actuators = markov.shape[2]
    probe_count = probes.shape[0]
    width_col = lax.axis_size("col")
    tile_rows = blocks_dev * width_col
    span = tile_rows + blocks_dev - 1
    total_rows = tile_rows * lax.axis_size("row") * sensors
    share_len = blocks_dev * sensors
    row_set = lax.all_gather(markov, "col", axis=0, tiled=True)
    next_rows = passed_along(row_set, "row", -1)
    joined = jnp.concatenate([row_set, next_rows], 0)
    first_block = lax.axis_index("col") * blocks_dev
    window = lax.dynamic_slice_in_dim(joined, first_block, span, 0)
    weights = probes.reshape(probe_count, blocks_dev, actuators)
    partial_value = jnp.zeros((probe_count, tile_rows, sensors), jnp.float32)
    for offset in range(blocks_dev):
        partial_value = partial_value + jnp.einsum(
            "qm,kpm->qkp",
            weights[:, offset],
            window[offset : offset + tile_rows],
            preferred_element_type=jnp.float32,
        )
    partial_value = partial_value.reshape(probe_count, tile_rows * sensors)
    response = lax.psum(partial_value, "col")
    squares = lax.psum(jnp.sum(response * response, axis=1, keepdims=True), "row")
    basis_full = (response * lax.rsqrt(squares / total_rows + 1e-06)).astype(jnp.bfloat16)
    basis_share = lax.dynamic_slice_in_dim(
        basis_full, lax.axis_index("col") * share_len, share_len, 1
    )
    basis_rows = basis_full.reshape(probe_count, tile_rows, sensors)
    pieces = [
        jnp.einsum(
            "qkp,kpm->qm",
            basis_rows,
            window[offset : offset + tile_rows],
            preferred_element_type=jnp.float32,
        )
        for offset in range(blocks_dev)
    ]
    local_sum = jnp.concatenate(pieces, 1)
    projected = lax.psum(local_sum, "row") * (1.0 / math.sqrt(total_rows))
    return (basis_share, projected)


def solution(mesh):
    return jax.shard_map(
        on_device,
        mesh=mesh,
        in_specs=(P(("row", "col"), None, None), P(None, "col")),
        out_specs=(P(None, ("row", "col")), P(None, "col")),
        check_vma=False,
    )
```

profile of v0, /device:TPU:0, one launch (start us, length us, event | category | flops | bytes accessed | tf_op | source)
XLA Modules:
  0.0 159.7 jit_solution(3367160880327190356)
XLA Ops:
  7.2 0.7 all-gather.2.cloned.1.call-update
  7.9 0.0 all-reduce.2.cloned.1.call-start
  7.9 21.1 %all-gather.2.cloned.1.call-done = bf16[16,512,64]{1,2,0:T(8,128)(2,1)} async-done(((bf16[4,512,64]{1,2,0:T(8,128)(2,1)}), bf16[16,512,64]{1,2,0:T(8,128)(2,1)}) %all-gather.2.cloned.1.call-update) | async-done | bytes 1048592 | tf_op jit(solution)/shard_map/all_gather | solution.py:25
  29.0 1.3 collective-permute-start
  30.3 0.8 reshape.13
  31.1 25.3 %collective-permute-done = bf16[16,512,64]{1,2,0:T(8,128)(2,1)S(1)} collective-permute-done((bf16[16,512,64]{1,2,0:T(8,128)(2,1)}, bf16[16,512,64]{1,2,0:T(8,128)(2,1)S(1)}, u32[]{:S(2)}, u32[]{:S(2)}) %collective-permute-start) | collective-permute-done | bytes 1048608 | tf_op jit(solution)/shard_map/ppermute | solution.py:12
  56.4 1.6 %fusion = bf16[19,512,64]{1,2,0:T(8,128)(2,1)S(1)} fusion(s32[]{:T(128)S(6)} %select_n.6, bf16[16,512,64]{1,2,0:T(8,128)(2,1)} %all-gather.2.cloned.1.call-done, bf16[16,512,64]{1,2,0:T(8,128)(2,1)S(1)} %collective-permute-done), kind=kLoop, calls=%fused_computation.2 | loop fusion | flops 622592 | bytes 3342340 | tf_op jit(solution)/shard_map/concatenate | solution.py:27
  58.0 0.3 fusion.11
  58.3 0.3 fusion.5
  58.5 0.3 fusion.8
  58.8 0.3 fusion.3
  59.1 0.8 copy.31
  59.9 33.3 %all-reduce.2.cloned.1.call-done = f32[16,8192]{1,0:T(8,128)} async-done(((f32[16,8192]{1,0:T(8,128)}), f32[16,8192]{1,0:T(8,128)}) %all-reduce.2.cloned.1.call-update) | async-done | bytes 524304 | tf_op jit(solution)/shard_map/psum | solution.py:40
  93.2 1.2 multiply_reduce_fusion
  94.5 21.4 %psum.22 = f32[16,1]{0,1:T(1,128)S(1)} all-reduce(f32[16,1]{0,1:T(1,128)S(1)} %bitcast.46), channel_id=1, replica_groups=mesh['row'=8,'col'=4] {'row'}, use_global_device_ids=true, to_apply=%region_2.0 | all-reduce | flops 16 | bytes 128 | tf_op jit(solution)/shard_map/psum | solution.py:41
  115.8 1.1 multiply_convert_fusion
  117.0 0.4 convolution_bitcast_fusion.3
  117.3 0.4 convolution_bitcast_fusion.2
  117.7 0.4 convolution_bitcast_fusion.1
  118.1 0.4 convolution_bitcast_fusion
  118.5 0.1 pad_maximum_fusion
  118.6 33.0 %psum.23 = f32[16,256]{1,0:T(8,128)S(1)} all-reduce(f32[16,256]{1,0:T(8,128)S(1)} %pad_maximum_fusion), channel_id=1, replica_groups=mesh['row'=8,'col'=4] {'row'}, use_global_device_ids=true, to_apply=%region_3.0 | all-reduce | flops 4096 | bytes 32768 | tf_op jit(solution)/shard_map/psum | solution.py:57
  151.6 0.6 broadcast_multiply_fusion
  152.2 0.6 constant_dynamic-slice_fusion
  (4 shorter events, 0.1 us)
Async XLA Ops:
  7.2 21.8 %all-gather.2.cloned.1.call-start = ((), (), s32[]{:S(2)}) async-start(), calls=%async_computation | async-start | bytes 1310720 | tf_op jit(solution)/shard_map/all_gather | solution.py:25
  7.9 85.3 %all-reduce.2.cloned.1.call-start = ((), (), s32[]{:S(2)}) async-start(), calls=%async_computation.1 | async-start | bytes 1048576 | tf_op jit(solution)/shard_map/psum | solution.py:40
  29.0 27.4 %collective-permute-start = (bf16[16,512,64]{1,2,0:T(8,128)(2,1)}, bf16[16,512,64]{1,2,0:T(8,128)(2,1)S(1)}, u32[]{:S(2)}, u32[]{:S(2)}) collective-permute-start(bf16[16,512,64]{1,2,0:T(8,128)(2,1)} %all-gather.2.cloned.1.call-done), channel_id=1, source_target_pairs={{4,0},{8,4},{12,8},{16,12},{20,16},{24,20},{28,24},{5,1},{9,5},{13... | collective-permute-start | bytes 3145736 | tf_op jit(solution)/shard_map/ppermute | solution.py:12
Sparse Core Ops, SparseCore 0:
  9.6 19.4 all-gather.1
  60.1 33.1 all-reduce.1
where the time goes:
time: 160 us
  waiting for transfers between devices  80.3 us (50%)
  blocking collectives  54.3 us (34%)
  between operations  14.1 us (9%)
  other arithmetic  4.69 us (3%)
  matrix products  2.57 us (2%)
  local copies, waits for them, and re-layouts  2.29 us (1%)
    psum x1, waiting for transfers between devices, on_device(): response = lax.psum(partial_value, 'col')  33.3 us
    psum x1, blocking collectives, on_device(): projected = lax.psum(local_sum, 'row') * (1.0 / math.sqrt(total_rows))  33 us
    ppermute x1, waiting for transfers between devices, passed_along(): return lax.ppermute(x, axis, pairs)  25.3 us
    psum x1, blocking collectives, on_device(): lax.psum(jnp.sum(response * response, axis=1, keepdims=True), 'row')  21.4 us
    all_gather x1, waiting for transfers between devices, on_device(): row_set = lax.all_gather(markov, 'col', axis=0, tiled=True)  21.1 us
  transfers between devices with their start and end apart: 3, of which 3 were waited for; matrix products, arithmetic and copies ran while one was open for 1% of the time, Pallas kernels for 0%

commit v1 on v0

v1 whole, which is shorter than its diff:
```python
import functools
import math

import jax
import jax.numpy as jnp
from jax import lax
from jax.experimental import pallas as pl
from jax.experimental.pallas import tpu as pltpu
from jax.sharding import PartitionSpec as P

MESH = pl.DeviceIdType.MESH
LANES = 128


def body(nr, nc, blocks_dev, markov, probes, basis_out, proj_out,
         pbuf, image_send, image_recv, image, back_send, back_recv,
         tile_acc, tile_send, tile_recv, all_send, all_recv,
         sem_ps, sem_pr, sem_is, sem_ir, sem_bs, sem_br, sem_ts, sem_tr, sem_as, sem_ar):
    f32, bf16 = jnp.float32, jnp.bfloat16
    q, tile = probes.shape
    sensors = markov.shape[1]
    act = tile // blocks_dev
    n = nr * nc
    row, col = lax.axis_index("row"), lax.axis_index("col")
    me = row * nc + col

    def at(d):
        return (d // nc, d % nc)

    def remote(src, dst, send, recv, device):
        return pltpu.make_async_remote_copy(src_ref=src, dst_ref=dst, send_sem=send, recv_sem=recv,
                                            device_id=device, device_id_type=MESH)

    barrier = pltpu.get_barrier_semaphore()

    def greet(device):
        pl.semaphore_signal(barrier, inc=1, device_id=device, device_id_type=MESH)

    for k in range(1, nc):
        greet((row, (col + k) % nc))
    for k in range(nc):
        @pl.when((row > 0) & (k >= col))
        def _():
            greet((row - 1, k))

        @pl.when((row < nr - 1) & (k <= col))
        def _():
            greet((row + 1, k))
    for k in range(nr):
        @pl.when((k > row + 1) | (k < row - 1))
        def _():
            greet((k, col))
    up = (row > 0).astype(jnp.int32)
    down = (row < nr - 1).astype(jnp.int32)
    pl.semaphore_wait(barrier, (nc - 1) + up * (nc - col) + down * (col + 1) + (nr - 1 - up - down))

    for k in range(1, nc):
        remote(probes, pbuf.at[col], sem_ps.at[k], sem_pr.at[col], (row, (col + k) % nc)).start()
    pbuf[col] = probes[...]
    for k in range(nc):
        @pl.when(col != k)
        def _():
            remote(probes, pbuf.at[k], sem_ps.at[0], sem_pr.at[k], (row, k)).wait_recv()

    lane = lax.broadcasted_iota(jnp.int32, (q, tile), 1)
    zero = jnp.zeros((q, tile), f32)
    parts = [pbuf[k].astype(f32) for k in range(nc)]
    rolled = [[p] + [pltpu.roll(p, act * u, 1) for u in range(1, blocks_dev)] for p in parts]

    def weights(t):
        rows = []
        for u in range(blocks_dev):
            upper = rolled[t][u] if t < nc else zero
            lower = rolled[t - 1][u] if t > 0 else zero
            rows.append(upper if u == 0 else jnp.where(lane < act * u, lower, upper))
        return jnp.concatenate(rows, 0).astype(bf16)

    def partial_image(t):
        return jnp.dot(weights(t), markov[...], preferred_element_type=f32)

    def rows_of(t):
        return pl.ds(q, (blocks_dev - 1) * q) if t == nc else pl.ds(0, blocks_dev * q)

    def image_copy(t, device):
        return remote(image_send.at[t - 1, rows_of(t)], image_recv.at[t - 1, rows_of(t)],
                      sem_is.at[t - 1], sem_ir.at[t - 1], device)

    def back_copy(t, device):
        return remote(back_send.at[rows_of(t)], back_recv.at[t - 1, rows_of(t)],
                      sem_bs.at[t - 1], sem_br.at[t - 1], device)

    for t in range(nc, 0, -1):
        @pl.when(me - t >= 0)
        def _():
            image_send[t - 1] = partial_image(t)
            image_copy(t, at(me - t)).start()
    image[...] = partial_image(0)
    for t in range(1, nc + 1):
        @pl.when(me + t < n)
        def _():
            image_copy(t, at(me + t)).wait_recv()
            image[rows_of(t)] += image_recv[t - 1, rows_of(t)]

    back_send[...] = image[...].astype(bf16)
    for t in range(nc, 0, -1):
        @pl.when(me + t < n)
        def _():
            back_copy(t, at(me + t)).start()

    squares = jnp.sum(image[...] * image[...], axis=1, keepdims=True)
    square = squares[0:q]
    for u in range(1, blocks_dev):
        square = square + squares[u * q : (u + 1) * q]
    square = jnp.broadcast_to(square, (q, LANES))
    tile_acc[...] = jnp.zeros_like(tile_acc)

    def project(t, part):
        prod = lax.dot_general(part, markov[...], (((1,), (1,)), ((), ())), preferred_element_type=f32)
        upper, lower = zero, zero
        for u in range(blocks_dev):
            piece = prod[u * q : (u + 1) * q]
            if u == 0:
                upper = upper + piece
                continue
            piece = pltpu.roll(piece, tile - act * u, 1)
            upper = upper + jnp.where(lane < tile - act * u, piece, 0.0)
            lower = lower + jnp.where(lane < tile - act * u, 0.0, piece)
        if t < nc:
            tile_acc[t] += upper
        if t > 0:
            tile_acc[t - 1] += lower

    def tile_copy(k, device):
        return remote(tile_send.at[k], tile_recv.at[col], sem_ts.at[k], sem_tr.at[col], device)

    project(0, back_send[...])
    for t in range(1, nc + 1):
        @pl.when(me - t >= 0)
        def _():
            back_copy(t, at(me - t)).wait_recv()
            part = back_recv[t - 1, rows_of(t)]
            if t == nc:
                part = jnp.concatenate([jnp.zeros((q, sensors), bf16), part], 0)
            project(t, part)
        tile_send[t - 1, :, 0:tile] = tile_acc[t - 1]
        tile_send[t - 1, :, tile : tile + LANES] = square

        @pl.when(col != t - 1)
        def _():
            tile_copy(t - 1, (row, t - 1)).start()

    tile_recv[col] = tile_send[col]
    for k in range(nc):
        @pl.when(col != k)
        def _():
            remote(tile_send.at[k], tile_recv.at[k], sem_ts.at[k], sem_tr.at[k], (row, k)).wait_recv()
    total = tile_recv[0]
    for k in range(1, nc):
        total = total + tile_recv[k]
    all_send[...] = total
    all_recv[row] = total
    for k in range(1, nr):
        remote(all_send, all_recv.at[row], sem_as.at[k], sem_ar.at[row], ((row + k) % nr, col)).start()
    for k in range(nr):
        @pl.when(row != k)
        def _():
            remote(all_send, all_recv.at[k], sem_as.at[0], sem_ar.at[k], (k, col)).wait_recv()
    total = all_recv[0]
    for k in range(1, nr):
        total = total + all_recv[k]

    count = n * blocks_dev * sensors
    scale = lax.rsqrt(total[:, tile : tile + 1] / count + 1e-06)
    proj_out[...] = total[:, 0:tile] * scale * (1.0 / math.sqrt(count))
    for u in range(blocks_dev):
        basis_out[:, u * sensors : (u + 1) * sensors] = (image[u * q : (u + 1) * q] * scale).astype(bf16)

    for k in range(1, nc):
        remote(probes, pbuf.at[col], sem_ps.at[k], sem_pr.at[col], (row, (col + k) % nc)).wait_send()
    for t in range(1, nc + 1):
        @pl.when(me - t >= 0)
        def _():
            image_copy(t, at(me - t)).wait_send()

        @pl.when(me + t < n)
        def _():
            back_copy(t, at(me + t)).wait_send()

        @pl.when(col != t - 1)
        def _():
            tile_copy(t - 1, (row, t - 1)).wait_send()
    for k in range(1, nr):
        remote(all_send, all_recv.at[row], sem_as.at[k], sem_ar.at[row], ((row + k) % nr, col)).wait_send()


def on_device(nr, nc, markov, probes):
    blocks_dev, sensors, act = markov.shape
    q, tile = probes.shape
    flat = jnp.transpose(markov, (0, 2, 1)).reshape(blocks_dev * act, sensors)
    vmem = pl.BlockSpec(memory_space=pltpu.VMEM)
    f32, bf16 = jnp.float32, jnp.bfloat16
    m = blocks_dev * q
    dma = pltpu.SemaphoreType.DMA
    return pl.pallas_call(
        functools.partial(body, nr, nc, blocks_dev),
        out_shape=(jax.ShapeDtypeStruct((q, blocks_dev * sensors), bf16), jax.ShapeDtypeStruct((q, tile), f32)),
        in_specs=[vmem, vmem],
        out_specs=(vmem, vmem),
        scratch_shapes=[
            pltpu.VMEM((nc, q, tile), bf16),
            pltpu.VMEM((nc, m, sensors), f32),
            pltpu.VMEM((nc, m, sensors), f32),
            pltpu.VMEM((m, sensors), f32),
            pltpu.VMEM((m, sensors), bf16),
            pltpu.VMEM((nc, m, sensors), bf16),
            pltpu.VMEM((nc, q, tile), f32),
            pltpu.VMEM((nc, q, tile + LANES), f32),
            pltpu.VMEM((nc, q, tile + LANES), f32),
            pltpu.VMEM((q, tile + LANES), f32),
            pltpu.VMEM((nr, q, tile + LANES), f32),
            dma((nc,)), dma((nc,)), dma((nc,)), dma((nc,)), dma((nc,)), dma((nc,)),
            dma((nc,)), dma((nc,)), dma((nr,)), dma((nr,)),
        ],
        compiler_params=pltpu.CompilerParams(
            collective_id=0, has_side_effects=True, vmem_limit_bytes=32 * 1024 * 1024
        ),
    )(flat, probes)


def solution(mesh):
    return jax.shard_map(
        functools.partial(on_device, mesh.shape["row"], mesh.shape["col"]),
        mesh=mesh,
        in_specs=(P(("row", "col"), None, None), P(None, "col")),
        out_specs=(P(None, ("row", "col")), P(None, "col")),
        check_vma=False,
    )
```

time: 160 us -> 39 us (0.24)
  the two profiles are of different devices: /device:TPU:0 before, /device:TPU:6 now
where the time goes in v1:
time: 39 us; the launch traced here: 38.8 us
  Pallas kernels  35.3 us (91%)
  local copies, waits for them, and re-layouts  2.88 us (7%)
  between operations  0.65 us (2%)
    pallas_call x1, Pallas kernels, on_device(): pl.pallas_call(functools.partial(body, nr, nc, blocks_dev), out_shape=(ja...  35.3 us
    unnamed x6, local copies, waits for them, and re-layouts  2.88 us

profile of v1, /device:TPU:6, one launch (start us, length us, event | category | flops | bytes accessed | tf_op | source)
XLA Modules:
  0.0 38.8 jit_solution(17249765983526492171)
XLA Ops:
  0.6 0.0 copy-start
  0.6 0.9 %copy-done = bf16[4,512,64]{1,2,0:T(8,128)(2,1)S(1)} copy-done((bf16[4,512,64]{1,2,0:T(8,128)(2,1)S(1)}, bf16[4,512,64]{1,2,0:T(8,128)(2,1)}, u32[]{:S(2)}) %copy-start) | copy-done | bytes 262168
  1.6 0.0 copy-start.1
  1.6 0.7 %copy-done.1 = bf16[16,256]{1,0:T(8,128)(2,1)S(1)} copy-done((bf16[16,256]{1,0:T(8,128)(2,1)S(1)}, bf16[16,256]{1,0:T(8,128)(2,1)}, u32[]{:S(2)}) %copy-start.1) | copy-done | bytes 8216
  2.3 35.3 %shard_map.41 = (bf16[16,2048]{1,0:T(8,128)(2,1)S(1)}, f32[16,256]{1,0:T(8,128)S(1)}) custom-call(bf16[256,512]{1,0:T(8,128)(2,1)S(1)} %bitcast.3, bf16[16,256]{1,0:T(8,128)(2,1)S(1)} %copy-done.1), custom_call_target="tpu_custom_call" | custom-call | tf_op jit(solution)/shard_map/pallas_call | solution.py:204
  37.6 0.6 %copy.6 = bf16[16,2048]{1,0:T(8,128)(2,1)} copy(bf16[16,2048]{1,0:T(8,128)(2,1)S(1)} %get-tuple-element.4) | data formatting | bytes 131072
  38.2 0.6 %copy.7 = f32[16,256]{1,0:T(8,128)} copy(f32[16,256]{1,0:T(8,128)S(1)} %get-tuple-element.5) | data formatting | bytes 32768
Async XLA Ops:
  0.6 1.0 %copy-start = (bf16[4,512,64]{1,2,0:T(8,128)(2,1)S(1)}, bf16[4,512,64]{1,2,0:T(8,128)(2,1)}, u32[]{:S(2)}) copy-start(bf16[4,512,64]{1,2,0:T(8,128)(2,1)} %param.2) | copy-start | bytes 786436
  1.6 0.7 %copy-start.1 = (bf16[16,256]{1,0:T(8,128)(2,1)S(1)}, bf16[16,256]{1,0:T(8,128)(2,1)}, u32[]{:S(2)}) copy-start(bf16[16,256]{1,0:T(8,128)(2,1)} %probes.1) | copy-start | bytes 24580

commit v2 on v1

v2 whole, which is shorter than its diff:
```python
import functools
import math

import jax
import jax.numpy as jnp
from jax import lax
from jax.experimental import pallas as pl
from jax.experimental.pallas import tpu as pltpu
from jax.sharding import PartitionSpec as P

MESH = pl.DeviceIdType.MESH
LANES = 128
CHUNKS = 4


def body(nr, nc, blocks_dev, chunks, markov, probes, basis_out, proj_out,
         window, pbuf, weight, image, tile_acc, tile_send, tile_recv, all_send, all_recv,
         sem_in, sem_ps, sem_pr, sem_own, sem_up, sem_relay, sem_fwd, sem_win,
         sem_ts, sem_tr, sem_as, sem_ar):
    f32, bf16 = jnp.float32, jnp.bfloat16
    q, tile = probes.shape
    sensors = markov.shape[1]
    act = tile // blocks_dev
    n = nr * nc
    pair = 2 if nr % 2 == 0 else 1
    row, col = lax.axis_index("row"), lax.axis_index("col")
    me = row * nc + col
    high, low = row // pair, row % pair
    odd = col % 2
    sibling = (row, col + 1 - 2 * odd)
    sent = []

    load_markov = pltpu.make_async_copy(markov, window.at[0], sem_in.at[0])
    load_probes = pltpu.make_async_copy(probes, pbuf.at[col], sem_in.at[1])
    load_markov.start()
    load_probes.start()

    def remote(src, dst, send, recv, device):
        return pltpu.make_async_remote_copy(src_ref=src, dst_ref=dst, send_sem=send, recv_sem=recv,
                                            device_id=device, device_id_type=MESH)

    def send(cond, copy):
        if cond is None:
            copy().start()
        else:
            @pl.when(cond)
            def _():
                copy().start()
        sent.append((cond, copy))

    barrier = pltpu.get_barrier_semaphore()

    def greet(device):
        pl.semaphore_signal(barrier, inc=1, device_id=device, device_id_type=MESH)

    for k in range(1, nc):
        greet((row, (col + k) % nc))
    if pair == 2:
        for k in range(nc):
            greet((row + 1 - 2 * low, k))
    groups = nr // pair
    for k in range(1, groups):
        greet(((high + k) % groups * pair + low, col))
    if pair == 2:
        step = 2 * low - 1
        lone = ((row + step >= 0) & (row + step < nr)).astype(jnp.int32)

        @pl.when(lone == 1)
        def _():
            greet((row + step, col))
        pl.semaphore_wait(barrier, nc - 1 + nc + groups - 1 + lone)
    else:
        pl.semaphore_wait(barrier, nc - 1 + groups - 1)

    def exists(t):
        return me + t < n

    def rows(v):
        size = blocks_dev * act // chunks
        return pl.ds(v * size, size)

    def win_copy(here, there, v, sem, device):
        return remote(window.at[here, rows(v)], window.at[there, rows(v)], sem, sem_win.at[there, v], device)

    def arrived(t, v):
        win_copy(t, t, v, sem_up.at[0], sibling).wait_recv()

    load_markov.wait()
    for v in range(chunks):
        send(row > 0, functools.partial(win_copy, 0, nc, v, sem_up.at[v], (row - 1, col)))
        for k in range(2, nc, 2):
            send(col >= k, functools.partial(win_copy, 0, k, v, sem_own.at[k, v], (row, col - k)))
    load_probes.wait()
    for k in range(1, nc):
        send(None, functools.partial(remote, pbuf.at[col], pbuf.at[col], sem_ps.at[k], sem_pr.at[col],
                                     (row, (col + k) % nc)))

    def forward(t, v):
        needed = (odd == 0) if t == nc else (odd == 1) if t == 0 else None
        cond = exists(t) if needed is None else exists(t) & needed
        there = t - 1 + 2 * odd
        send(cond, functools.partial(win_copy, t, there, v, sem_fwd.at[t, v], sibling))

    for v in range(chunks):
        forward(0, v)

    for k in range(nc):
        @pl.when(col != k)
        def _():
            remote(pbuf.at[k], pbuf.at[k], sem_ps.at[0], sem_pr.at[k], sibling).wait_recv()
    lane = lax.broadcasted_iota(jnp.int32, (q, tile), 1)
    zero = jnp.zeros((q, tile), f32)
    parts = [pbuf[k].astype(f32) for k in range(nc)]
    rolled = [[p] + [pltpu.roll(p, act * u, 1) for u in range(1, blocks_dev)] for p in parts]
    for t in range(nc + 1):
        for u in range(blocks_dev):
            upper = rolled[t][u] if t < nc else zero
            lower = rolled[t - 1][u] if t > 0 else zero
            part = upper if u == 0 else jnp.where(lane < act * u, lower, upper)
            weight[t, u * q : (u + 1) * q] = part.astype(bf16)

    def add_image(t):
        image[...] += jnp.dot(weight[t], window[t], preferred_element_type=f32)

    image[...] = jnp.dot(weight[0], window[0], preferred_element_type=f32)

    for v in range(chunks):
        @pl.when(exists(nc))
        def _():
            arrived(nc, v)
        for k in range(2, nc, 2):
            send(exists(nc) & (col + k < nc),
                 functools.partial(win_copy, nc, nc - k, v, sem_relay.at[k, v], (row, col + k)))
        forward(nc, v)
        for t in range(2, nc, 2):
            @pl.when(col + t < nc)
            def _():
                arrived(t, v)
                win_copy(t, t - 1 + 2 * odd, v, sem_fwd.at[t, v], sibling).start()

    @pl.when(exists(nc))
    def _():
        add_image(nc)
    for v in range(chunks):
        for t in range(2, nc, 2):
            @pl.when(exists(t) & (col + t >= nc))
            def _():
                arrived(t, v)
                win_copy(t, t - 1 + 2 * odd, v, sem_fwd.at[t, v], sibling).start()
            sent.append((exists(t), functools.partial(
                win_copy, t, t - 1 + 2 * odd, v, sem_fwd.at[t, v], sibling)))
    for t in [*range(2, nc, 2), *range(1, nc, 2)]:
        @pl.when(exists(t))
        def _():
            if t % 2 == 1:
                for v in range(chunks):
                    arrived(t, v)
            add_image(t)

    squares = jnp.sum(image[...] * image[...], axis=1, keepdims=True)
    square = squares[0:q]
    for u in range(1, blocks_dev):
        square = square + squares[u * q : (u + 1) * q]
    square = jnp.broadcast_to(square, (q, LANES))
    tile_acc[...] = jnp.zeros_like(tile_acc)
    image16 = image[...].astype(bf16)

    def project(t):
        prod = lax.dot_general(image16, window[t], (((1,), (1,)), ((), ())), preferred_element_type=f32)
        upper, lower = zero, zero
        for u in range(blocks_dev):
            piece = prod[u * q : (u + 1) * q]
            if u == 0:
                upper = upper + piece
                continue
            piece = pltpu.roll(piece, tile - act * u, 1)
            upper = upper + jnp.where(lane < tile - act * u, piece, 0.0)
            lower = lower + jnp.where(lane < tile - act * u, 0.0, piece)
        if t < nc:
            tile_acc[t] += upper
        if t > 0:
            tile_acc[t - 1] += lower

    def tile_copy(k, r, sem):
        place = low * nc + col
        return remote(tile_send.at[k], tile_recv.at[place], sem, sem_tr.at[place], (r, k))

    project(0)
    for t in range(1, nc + 1):
        @pl.when(exists(t))
        def _():
            project(t)
        tile_send[t - 1, :, 0:tile] = tile_acc[t - 1]
        tile_send[t - 1, :, tile : tile + LANES] = square
        if pair == 2:
            send(None, functools.partial(tile_copy, t - 1, row + 1 - 2 * low, sem_ts.at[1, t - 1]))
        send(col != t - 1, functools.partial(tile_copy, t - 1, row, sem_ts.at[0, t - 1]))
    tile_recv[low * nc + col] = tile_send[col]
    total = None
    for k in range(pair * nc):
        @pl.when(low * nc + col != k)
        def _():
            remote(tile_recv.at[k], tile_recv.at[k], sem_ts.at[0, 0], sem_tr.at[k], sibling).wait_recv()
    total = tile_recv[0]
    for k in range(1, pair * nc):
        total = total + tile_recv[k]
    all_send[...] = total
    all_recv[high] = total
    for k in range(1, groups):
        send(None, functools.partial(remote, all_send, all_recv.at[high], sem_as.at[k], sem_ar.at[high],
                                     ((high + k) % groups * pair + low, col)))
    for k in range(groups):
        @pl.when(high != k)
        def _():
            remote(all_send, all_recv.at[k], sem_as.at[0], sem_ar.at[k], sibling).wait_recv()
    total = all_recv[0]
    for k in range(1, groups):
        total = total + all_recv[k]

    count = n * blocks_dev * sensors
    scale = lax.rsqrt(total[:, tile : tile + 1] / count + 1e-06)
    proj_out[...] = total[:, 0:tile] * scale * (1.0 / math.sqrt(count))
    for u in range(blocks_dev):
        basis_out[:, u * sensors : (u + 1) * sensors] = (image[u * q : (u + 1) * q] * scale).astype(bf16)

    for cond, copy in sent:
        if cond is None:
            copy().wait_send()
        else:
            @pl.when(cond)
            def _():
                copy().wait_send()


def on_device(nr, nc, markov, probes):
    blocks_dev, sensors, act = markov.shape
    q, tile = probes.shape
    flat = jnp.transpose(markov, (0, 2, 1)).reshape(blocks_dev * act, sensors)
    vmem, anywhere = pl.BlockSpec(memory_space=pltpu.VMEM), pl.BlockSpec(memory_space=pl.ANY)
    f32, bf16 = jnp.float32, jnp.bfloat16
    m = blocks_dev * q
    chunks = CHUNKS
    dma = pltpu.SemaphoreType.DMA
    return pl.pallas_call(
        functools.partial(body, nr, nc, blocks_dev, chunks),
        out_shape=(jax.ShapeDtypeStruct((q, blocks_dev * sensors), bf16), jax.ShapeDtypeStruct((q, tile), f32)),
        in_specs=[anywhere, anywhere],
        out_specs=(vmem, vmem),
        scratch_shapes=[
            pltpu.VMEM((nc + 1, blocks_dev * act, sensors), bf16),
            pltpu.VMEM((nc, q, tile), bf16),
            pltpu.VMEM((nc + 1, m, tile), bf16),
            pltpu.VMEM((m, sensors), f32),
            pltpu.VMEM((nc, q, tile), f32),
            pltpu.VMEM((nc, q, tile + LANES), f32),
            pltpu.VMEM((2 * nc, q, tile + LANES), f32),
            pltpu.VMEM((q, tile + LANES), f32),
            pltpu.VMEM((nr, q, tile + LANES), f32),
            dma((2,)), dma((nc,)), dma((nc,)), dma((nc, chunks)), dma((chunks,)), dma((nc, chunks)),
            dma((nc + 1, chunks)), dma((nc + 1, chunks)),
            dma((2, nc)), dma((2 * nc,)), dma((nr,)), dma((nr,)),
        ],
        compiler_params=pltpu.CompilerParams(
            collective_id=0, has_side_effects=True, vmem_limit_bytes=32 * 1024 * 1024
        ),
    )(flat, probes)


def solution(mesh):
    return jax.shard_map(
        functools.partial(on_device, mesh.shape["row"], mesh.shape["col"]),
        mesh=mesh,
        in_specs=(P(("row", "col"), None, None), P(None, "col")),
        out_specs=(P(None, ("row", "col")), P(None, "col")),
        check_vma=False,
    )
```

time: 39 us -> 35.4 us (0.908)
  the two profiles are of different devices: /device:TPU:6 before, /device:TPU:0 now
where the time goes in v2:
time: 35.4 us; the launch traced here: 35.1 us
  Pallas kernels  31.6 us (89%)
  local copies, waits for them, and re-layouts  2.88 us (8%)
  between operations  0.65 us (2%)
    pallas_call x1, Pallas kernels, on_device(): pl.pallas_call(functools.partial(body, nr, nc, blocks_dev, chunks), out_s...  31.6 us
    unnamed x6, local copies, waits for them, and re-layouts  2.88 us

profile of v2, /device:TPU:0, one launch (start us, length us, event | category | flops | bytes accessed | tf_op | source)
XLA Modules:
  0.0 35.1 jit_solution(11558612090785586847)
XLA Ops:
  0.6 0.0 copy-start
  0.6 0.9 %copy-done = bf16[4,512,64]{1,2,0:T(8,128)(2,1)S(1)} copy-done((bf16[4,512,64]{1,2,0:T(8,128)(2,1)S(1)}, bf16[4,512,64]{1,2,0:T(8,128)(2,1)}, u32[]{:S(2)}) %copy-start) | copy-done | bytes 262168
  1.6 0.0 copy-start.1
  1.6 0.7 %copy-done.1 = bf16[16,256]{1,0:T(8,128)(2,1)S(1)} copy-done((bf16[16,256]{1,0:T(8,128)(2,1)S(1)}, bf16[16,256]{1,0:T(8,128)(2,1)}, u32[]{:S(2)}) %copy-start.1) | copy-done | bytes 8216
  2.3 31.6 %shard_map.41 = (bf16[16,2048]{1,0:T(8,128)(2,1)S(1)}, f32[16,256]{1,0:T(8,128)S(1)}) custom-call(bf16[256,512]{1,0:T(8,128)(2,1)S(1)} %bitcast.3, bf16[16,256]{1,0:T(8,128)(2,1)S(1)} %copy-done.1), custom_call_target="tpu_custom_call" | custom-call | tf_op jit(solution)/shard_map/pallas_call | solution.py:244
  33.9 0.6 %copy.6 = bf16[16,2048]{1,0:T(8,128)(2,1)} copy(bf16[16,2048]{1,0:T(8,128)(2,1)S(1)} %get-tuple-element.4) | data formatting | bytes 131072
  34.5 0.6 %copy.7 = f32[16,256]{1,0:T(8,128)} copy(f32[16,256]{1,0:T(8,128)S(1)} %get-tuple-element.5) | data formatting | bytes 32768
Async XLA Ops:
  0.6 1.0 %copy-start = (bf16[4,512,64]{1,2,0:T(8,128)(2,1)S(1)}, bf16[4,512,64]{1,2,0:T(8,128)(2,1)}, u32[]{:S(2)}) copy-start(bf16[4,512,64]{1,2,0:T(8,128)(2,1)} %param.2) | copy-start | bytes 786436
  1.6 0.7 %copy-start.1 = (bf16[16,256]{1,0:T(8,128)(2,1)S(1)}, bf16[16,256]{1,0:T(8,128)(2,1)}, u32[]{:S(2)}) copy-start(bf16[16,256]{1,0:T(8,128)(2,1)} %probes.1) | copy-start | bytes 24580

commit v3 on v2

--- a/solution.py
+++ b/solution.py
@@ -10,7 +10,7 @@
 
 MESH = pl.DeviceIdType.MESH
 LANES = 128
-CHUNKS = 4
+DIRECT = 4
 
 
 def body(nr, nc, blocks_dev, chunks, markov, probes, basis_out, proj_out,
@@ -65,10 +65,16 @@
         step = 2 * low - 1
         lone = ((row + step >= 0) & (row + step < nr)).astype(jnp.int32)
 
-        @pl.when(lone == 1)
-        def _():
-            greet((row + step, col))
-        pl.semaphore_wait(barrier, nc - 1 + nc + groups - 1 + lone)
+        met = 0
+        for k in range(0, nc, 2):
+            other = col - step * k
+            meets = lone * ((other >= 0) & (other < nc)).astype(jnp.int32)
+            met = met + meets
+
+            @pl.when(meets == 1)
+            def _():
+                greet((row + step, other))
+        pl.semaphore_wait(barrier, nc - 1 + nc + groups - 1 + met)
     else:
         pl.semaphore_wait(barrier, nc - 1 + groups - 1)
 
@@ -85,9 +91,20 @@
     def arrived(t, v):
         win_copy(t, t, v, sem_up.at[0], sibling).wait_recv()
 
+    def up_needs(below, v):
+        cond = (below > 0) & (below < nr)
+        return cond & (col < nc - 1) if v == chunks - 1 else cond
+
+    @pl.when(col == nc - 1)
+    def _():
+        window[nc, (chunks - 1) * act :] = jnp.zeros((act, sensors), bf16)
     load_markov.wait()
     for v in range(chunks):
-        send(row > 0, functools.partial(win_copy, 0, nc, v, sem_up.at[v], (row - 1, col)))
+        send(up_needs(row, v), functools.partial(win_copy, 0, nc, v, sem_up.at[v], (row - 1, col)))
+        if v < DIRECT:
+            for k in range(2, nc, 2):
+                send((row > 0) & (col + k < nc),
+                     functools.partial(win_copy, 0, nc - k, v, sem_relay.at[k, v], (row - 1, col + k)))
         for k in range(2, nc, 2):
             send(col >= k, functools.partial(win_copy, 0, k, v, sem_own.at[k, v], (row, col - k)))
     load_probes.wait()
@@ -124,11 +141,11 @@
 
     image[...] = jnp.dot(weight[0], window[0], preferred_element_type=f32)
 
-    for v in range(chunks):
-        @pl.when(exists(nc))
+    for v in reversed(range(chunks)):
+        @pl.when(up_needs(row + 1, v))
         def _():
             arrived(nc, v)
-        for k in range(2, nc, 2):
+        for k in range(2, nc, 2) if v >= DIRECT else ():
             send(exists(nc) & (col + k < nc),
                  functools.partial(win_copy, nc, nc - k, v, sem_relay.at[k, v], (row, col + k)))
         forward(nc, v)
@@ -239,7 +256,7 @@
     vmem, anywhere = pl.BlockSpec(memory_space=pltpu.VMEM), pl.BlockSpec(memory_space=pl.ANY)
     f32, bf16 = jnp.float32, jnp.bfloat16
     m = blocks_dev * q
-    chunks = CHUNKS
+    chunks = blocks_dev
     dma = pltpu.SemaphoreType.DMA
     return pl.pallas_call(
         functools.partial(body, nr, nc, blocks_dev, chunks),

time: 35.4 us -> 33.2 us (0.938)
  Pallas kernels: 31.6 us -> 29.5 us
    pallas_call x1, Pallas kernels: 31.6 us -> 29.5 us  [on_device(): pl.pallas_call(functools.partial(body, nr, nc, blocks_dev, chunks), out_s...]
where the time goes in v3:
time: 33.2 us; the launch traced here: 33 us
  Pallas kernels  29.5 us (89%)
  local copies, waits for them, and re-layouts  2.88 us (9%)
  between operations  0.65 us (2%)
    pallas_call x1, Pallas kernels, on_device(): pl.pallas_call(functools.partial(body, nr, nc, blocks_dev, chunks), out_s...  29.5 us
    unnamed x6, local copies, waits for them, and re-layouts  2.88 us

profile of v3, /device:TPU:0, one launch (start us, length us, event | category | flops | bytes accessed | tf_op | source)
XLA Modules:
  0.0 33.0 jit_solution(7429890051853971559)
XLA Ops:
  0.6 0.0 copy-start
  0.6 0.9 %copy-done = bf16[4,512,64]{1,2,0:T(8,128)(2,1)S(1)} copy-done((bf16[4,512,64]{1,2,0:T(8,128)(2,1)S(1)}, bf16[4,512,64]{1,2,0:T(8,128)(2,1)}, u32[]{:S(2)}) %copy-start) | copy-done | bytes 262168
  1.6 0.0 copy-start.1
  1.6 0.7 %copy-done.1 = bf16[16,256]{1,0:T(8,128)(2,1)S(1)} copy-done((bf16[16,256]{1,0:T(8,128)(2,1)S(1)}, bf16[16,256]{1,0:T(8,128)(2,1)}, u32[]{:S(2)}) %copy-start.1) | copy-done | bytes 8216
  2.3 29.5 %shard_map.41 = (bf16[16,2048]{1,0:T(8,128)(2,1)S(1)}, f32[16,256]{1,0:T(8,128)S(1)}) custom-call(bf16[256,512]{1,0:T(8,128)(2,1)S(1)} %bitcast.3, bf16[16,256]{1,0:T(8,128)(2,1)S(1)} %copy-done.1), custom_call_target="tpu_custom_call" | custom-call | tf_op jit(solution)/shard_map/pallas_call | solution.py:261
  31.8 0.6 %copy.6 = bf16[16,2048]{1,0:T(8,128)(2,1)} copy(bf16[16,2048]{1,0:T(8,128)(2,1)S(1)} %get-tuple-element.4) | data formatting | bytes 131072
  32.4 0.6 %copy.7 = f32[16,256]{1,0:T(8,128)} copy(f32[16,256]{1,0:T(8,128)S(1)} %get-tuple-element.5) | data formatting | bytes 32768
Async XLA Ops:
  0.6 1.0 %copy-start = (bf16[4,512,64]{1,2,0:T(8,128)(2,1)S(1)}, bf16[4,512,64]{1,2,0:T(8,128)(2,1)}, u32[]{:S(2)}) copy-start(bf16[4,512,64]{1,2,0:T(8,128)(2,1)} %param.2) | copy-start | bytes 786436
  1.6 0.7 %copy-start.1 = (bf16[16,256]{1,0:T(8,128)(2,1)S(1)}, bf16[16,256]{1,0:T(8,128)(2,1)}, u32[]{:S(2)}) copy-start(bf16[16,256]{1,0:T(8,128)(2,1)} %probes.1) | copy-start | bytes 24580

commit v4 on v3

--- a/solution.py
+++ b/solution.py
@@ -10,11 +10,11 @@
 
 MESH = pl.DeviceIdType.MESH
 LANES = 128
-DIRECT = 4
+DIRECT = 3
 
 
 def body(nr, nc, blocks_dev, chunks, markov, probes, basis_out, proj_out,
-         window, pbuf, weight, image, tile_acc, tile_send, tile_recv, all_send, all_recv,
+         window, through, sem_ths, sem_thr, pbuf, weight, image, tile_acc, tile_send, tile_recv, all_send, all_recv,
          sem_in, sem_ps, sem_pr, sem_own, sem_up, sem_relay, sem_fwd, sem_win,
          sem_ts, sem_tr, sem_as, sem_ar):
     f32, bf16 = jnp.float32, jnp.bfloat16
@@ -98,7 +98,17 @@
     @pl.when(col == nc - 1)
     def _():
         window[nc, (chunks - 1) * act :] = jnp.zeros((act, sensors), bf16)
+    def through_copy(k, v, device):
+        return remote(window.at[0, rows(v)], through.at[k, rows(v)], sem_ths.at[k, v], sem_thr.at[k, v], device)
+
+    def relay_copy(k, v):
+        return remote(through.at[k, rows(v)], window.at[nc - k, rows(v)], sem_relay.at[k, v],
+                      sem_win.at[nc - k, v], (row - 1, col))
+
     load_markov.wait()
+    for v in range(DIRECT, chunks):
+        for k in range(2, nc, 2):
+            send((row > 0) & (col + k < nc), functools.partial(through_copy, k, v, (row, col + k)))
     for v in range(chunks):
         send(up_needs(row, v), functools.partial(win_copy, 0, nc, v, sem_up.at[v], (row - 1, col)))
         if v < DIRECT:
@@ -141,13 +151,18 @@
 
     image[...] = jnp.dot(weight[0], window[0], preferred_element_type=f32)
 
+    for v in range(DIRECT, chunks):
+        for k in range(2, nc, 2):
+            @pl.when((row > 0) & (col >= k))
+            def _():
+                through_copy(k, v, sibling).wait_recv()
+                relay_copy(k, v).start()
+            sent.append(((row > 0) & (col >= k), functools.partial(relay_copy, k, v)))
+
     for v in reversed(range(chunks)):
         @pl.when(up_needs(row + 1, v))
         def _():
             arrived(nc, v)
-        for k in range(2, nc, 2) if v >= DIRECT else ():
-            send(exists(nc) & (col + k < nc),
-                 functools.partial(win_copy, nc, nc - k, v, sem_relay.at[k, v], (row, col + k)))
         forward(nc, v)
         for t in range(2, nc, 2):
             @pl.when(col + t < nc)
@@ -265,6 +280,8 @@
         out_specs=(vmem, vmem),
         scratch_shapes=[
             pltpu.VMEM((nc + 1, blocks_dev * act, sensors), bf16),
+            pltpu.VMEM((nc, blocks_dev * act, sensors), bf16),
+            dma((nc, chunks)), dma((nc, chunks)),
             pltpu.VMEM((nc, q, tile), bf16),
             pltpu.VMEM((nc + 1, m, tile), bf16),
             pltpu.VMEM((m, sensors), f32),

time: 33.2 us -> 32.9 us (level)
  Pallas kernels: 29.5 us -> 29.1 us
    pallas_call x1, Pallas kernels: 29.5 us -> 29.1 us  [on_device(): pl.pallas_call(functools.partial(body, nr, nc, blocks_dev, chunks), out_s...]
where the time goes in v4:
time: 32.9 us; the launch traced here: 32.6 us
  Pallas kernels  29.1 us (88%)
  local copies, waits for them, and re-layouts  2.88 us (9%)
  between operations  0.65 us (2%)
    pallas_call x1, Pallas kernels, on_device(): pl.pallas_call(functools.partial(body, nr, nc, blocks_dev, chunks), out_s...  29.1 us
    unnamed x6, local copies, waits for them, and re-layouts  2.88 us

profile of v4, /device:TPU:0, one launch (start us, length us, event | category | flops | bytes accessed | tf_op | source)
XLA Modules:
  0.0 32.6 jit_solution(17620241584741000856)
XLA Ops:
  0.6 0.0 copy-start
  0.6 0.9 %copy-done = bf16[4,512,64]{1,2,0:T(8,128)(2,1)S(1)} copy-done((bf16[4,512,64]{1,2,0:T(8,128)(2,1)S(1)}, bf16[4,512,64]{1,2,0:T(8,128)(2,1)}, u32[]{:S(2)}) %copy-start) | copy-done | bytes 262168
  1.6 0.0 copy-start.1
  1.6 0.7 %copy-done.1 = bf16[16,256]{1,0:T(8,128)(2,1)S(1)} copy-done((bf16[16,256]{1,0:T(8,128)(2,1)S(1)}, bf16[16,256]{1,0:T(8,128)(2,1)}, u32[]{:S(2)}) %copy-start.1) | copy-done | bytes 8216
  2.3 29.1 %shard_map.41 = (bf16[16,2048]{1,0:T(8,128)(2,1)S(1)}, f32[16,256]{1,0:T(8,128)S(1)}) custom-call(bf16[256,512]{1,0:T(8,128)(2,1)S(1)} %bitcast.3, bf16[16,256]{1,0:T(8,128)(2,1)S(1)} %copy-done.1), custom_call_target="tpu_custom_call" | custom-call | tf_op jit(solution)/shard_map/pallas_call | solution.py:276
  31.4 0.6 %copy.6 = bf16[16,2048]{1,0:T(8,128)(2,1)} copy(bf16[16,2048]{1,0:T(8,128)(2,1)S(1)} %get-tuple-element.4) | data formatting | bytes 131072
  32.0 0.6 %copy.7 = f32[16,256]{1,0:T(8,128)} copy(f32[16,256]{1,0:T(8,128)S(1)} %get-tuple-element.5) | data formatting | bytes 32768
Async XLA Ops:
  0.6 1.0 %copy-start = (bf16[4,512,64]{1,2,0:T(8,128)(2,1)S(1)}, bf16[4,512,64]{1,2,0:T(8,128)(2,1)}, u32[]{:S(2)}) copy-start(bf16[4,512,64]{1,2,0:T(8,128)(2,1)} %param.2) | copy-start | bytes 786436
  1.6 0.7 %copy-start.1 = (bf16[16,256]{1,0:T(8,128)(2,1)S(1)}, bf16[16,256]{1,0:T(8,128)(2,1)}, u32[]{:S(2)}) copy-start(bf16[16,256]{1,0:T(8,128)(2,1)} %probes.1) | copy-start | bytes 24580

commit v5 on v4

--- a/solution.py
+++ b/solution.py
@@ -53,14 +53,14 @@
     def greet(device):
         pl.semaphore_signal(barrier, inc=1, device_id=device, device_id_type=MESH)
 
-    for k in range(1, nc):
-        greet((row, (col + k) % nc))
+    groups = nr // pair
+    for k in range(1, groups):
+        greet(((high + k) % groups * pair + low, col))
     if pair == 2:
         for k in range(nc):
             greet((row + 1 - 2 * low, k))
-    groups = nr // pair
-    for k in range(1, groups):
-        greet(((high + k) % groups * pair + low, col))
+    for k in range(1, nc):
+        greet((row, (col + k) % nc))
     if pair == 2:
         step = 2 * low - 1
         lone = ((row + step >= 0) & (row + step < nr)).astype(jnp.int32)

time: 32.9 us -> 32.9 us (level)
  no operation moved by 1% of the time
where the time goes in v5:
time: 32.9 us; the launch traced here: 32.7 us
  Pallas kernels  29.2 us (89%)
  local copies, waits for them, and re-layouts  2.88 us (9%)
  between operations  0.65 us (2%)
    pallas_call x1, Pallas kernels, on_device(): pl.pallas_call(functools.partial(body, nr, nc, blocks_dev, chunks), out_s...  29.2 us
    unnamed x6, local copies, waits for them, and re-layouts  2.88 us

profile of v5, /device:TPU:0, one launch (start us, length us, event | category | flops | bytes accessed | tf_op | source)
XLA Modules:
  0.0 32.7 jit_solution(14830457389544228877)
XLA Ops:
  0.6 0.0 copy-start
  0.6 0.9 %copy-done = bf16[4,512,64]{1,2,0:T(8,128)(2,1)S(1)} copy-done((bf16[4,512,64]{1,2,0:T(8,128)(2,1)S(1)}, bf16[4,512,64]{1,2,0:T(8,128)(2,1)}, u32[]{:S(2)}) %copy-start) | copy-done | bytes 262168
  1.6 0.0 copy-start.1
  1.6 0.7 %copy-done.1 = bf16[16,256]{1,0:T(8,128)(2,1)S(1)} copy-done((bf16[16,256]{1,0:T(8,128)(2,1)S(1)}, bf16[16,256]{1,0:T(8,128)(2,1)}, u32[]{:S(2)}) %copy-start.1) | copy-done | bytes 8216
  2.3 29.2 %shard_map.41 = (bf16[16,2048]{1,0:T(8,128)(2,1)S(1)}, f32[16,256]{1,0:T(8,128)S(1)}) custom-call(bf16[256,512]{1,0:T(8,128)(2,1)S(1)} %bitcast.3, bf16[16,256]{1,0:T(8,128)(2,1)S(1)} %copy-done.1), custom_call_target="tpu_custom_call" | custom-call | tf_op jit(solution)/shard_map/pallas_call | solution.py:276
  31.5 0.6 %copy.6 = bf16[16,2048]{1,0:T(8,128)(2,1)} copy(bf16[16,2048]{1,0:T(8,128)(2,1)S(1)} %get-tuple-element.4) | data formatting | bytes 131072
  32.1 0.6 %copy.7 = f32[16,256]{1,0:T(8,128)} copy(f32[16,256]{1,0:T(8,128)S(1)} %get-tuple-element.5) | data formatting | bytes 32768
Async XLA Ops:
  0.6 1.0 %copy-start = (bf16[4,512,64]{1,2,0:T(8,128)(2,1)S(1)}, bf16[4,512,64]{1,2,0:T(8,128)(2,1)}, u32[]{:S(2)}) copy-start(bf16[4,512,64]{1,2,0:T(8,128)(2,1)} %param.2) | copy-start | bytes 786436
  1.6 0.7 %copy-start.1 = (bf16[16,256]{1,0:T(8,128)(2,1)S(1)}, bf16[16,256]{1,0:T(8,128)(2,1)}, u32[]{:S(2)}) copy-start(bf16[16,256]{1,0:T(8,128)(2,1)} %probes.1) | copy-start | bytes 24580
